TPU v7x, 256 devices: a whole 4x4x8 slice. The times are simulated.
256 devices in a mesh: lat: 16 (over z, core), lon: 16 (over x, y).
Axes of the slice: x: 4, y: 4, z: 8, core: 2. Of those that a mesh axis runs over, the one named last changes fastest.
Arguments:
- grid_values: float32 [768, 1440, 256], P('lat', 'lon'), may hold values from -6 to 6
- wave_table: int32 [512], replicated, may hold values from 0 to 511, as said below
- legendre_basis: float32 [512, 384, 720], P(('lat', 'lon')), as said below
Outputs:
- coefficients: float32 [512, 720, 512], P(('lat', 'lon'))
Inputs may be any that keep to these rules, and one draw needn't show every extreme that they name: `wave_table`: a permutation of the wavenumbers 0 to 511. legendre_basis[r, j, l] is zero wherever l < wave_table[r].
All inputs are finite; a program needn't handle non-finite values.
Results may differ from a plain program's by a relative error of at most 0.0003.
Values sent between devices are 32-bit elements; how exact they have to be, the bound alone decides.
A program may use at most 128 MiB of HBM per device.

v0:
```python
import math

import jax
import jax.numpy as jnp
from jax import lax
from jax.sharding import PartitionSpec as P

highest = lax.Precision.HIGHEST


def fourier_matrix(columns, point_count, circle):
    points = jnp.arange(point_count, dtype=jnp.int32)
    product = points[:, None] * columns[None, :] % circle
    angles = product.astype(jnp.float32) * (2.0 * math.pi / circle)
    factor = 1.0 / math.sqrt(circle)
    return jnp.stack([jnp.cos(angles) * factor, -jnp.sin(angles) * factor], axis=1)


def on_device(grid_values, wave_table, legendre_basis):
    lat_count = lax.axis_size("lat")
    lon_count = lax.axis_size("lon")
    slot_total = wave_table.shape[0]
    slot_dev = slot_total // (lat_count * lon_count)
    column_order = wave_table.reshape(lat_count, lon_count, slot_dev).transpose(1, 0, 2).reshape(-1)
    circles = lax.all_to_all(grid_values, "lon", split_axis=0, concat_axis=1, tiled=True)
    circle = circles.shape[1]
    matrix = fourier_matrix(column_order, circle, circle)
    spectrum = jnp.einsum("anc,nsk->kasc", circles, matrix, precision=highest)
    wave_blocks = lax.all_to_all(spectrum, "lon", split_axis=0, concat_axis=1, tiled=True)
    gathered = lax.all_to_all(wave_blocks, "lat", split_axis=0, concat_axis=1, tiled=True)
    half_rows = gathered.shape[1] // 2
    northern = gathered[:, :half_rows]
    southern = jnp.flip(gathered[:, half_rows:], axis=1)
    even_part = northern + southern
    odd_part = northern - southern
    slot_first = (lax.axis_index("lat") * lon_count + lax.axis_index("lon")) * slot_dev
    waves = lax.dynamic_slice_in_dim(wave_table, slot_first, slot_dev)
    parity = waves % 2
    degree_count = legendre_basis.shape[2]
    half_degrees = degree_count // 2
    paired = legendre_basis.reshape(slot_dev, half_rows, half_degrees, 2)
    flag = (parity == 0)[:, None, None]
    same_rows = jnp.where(flag, paired[..., 0], paired[..., 1])
    other_rows = jnp.where(flag, paired[..., 1], paired[..., 0])
    same_sums = jnp.einsum("tjk,tjsc->tksc", same_rows, even_part, precision=highest)
    other_sums = jnp.einsum("tjk,tjsc->tksc", other_rows, odd_part, precision=highest)
    wide_flag = (parity == 0)[:, None, None, None, None]
    ordered = jnp.where(
        wide_flag, jnp.stack([same_sums, other_sums], 2), jnp.stack([other_sums, same_sums], 2)
    )
    return ordered.reshape(slot_dev, degree_count, -1)


def solution(mesh):
    placed = (P("lat", "lon", None), P(), P(("lat", "lon"), None, None))
    return jax.shard_map(
        on_device,
        mesh=mesh,
        in_specs=placed,
        out_specs=P(("lat", "lon"), None, None),
        check_vma=False,
    )
```

profile of v0, /device:TPU:1, one launch (start us, length us, event | category | flops | bytes accessed | tf_op | source)
XLA Modules:
  0.0 297.9 jit_solution(16884065168811281621)
XLA Ops:
  0.0 7.0 %copy.53 = f32[48,90,256]{2,1,0:T(8,128)} copy(f32[48,90,256]{2,0,1:T(8,128)} %param.3) | data formatting | bytes 8847360 | tf_op args[0]
  7.0 7.8 %all-to-all-start = ((f32[48,90,256]{2,1,0:T(8,128)}), f32[48,90,256]{2,1,0:T(8,128)}, u32[]{:S(2)}, u32[]{:S(2)}) async-start(f32[48,90,256]{2,1,0:T(8,128)} %copy.53), calls=%async_computation | async-start | bytes 9437184 | tf_op jit(solution)/shard_map/all_to_all | solution.py:25
  14.8 0.0 copy-done.4
  14.8 0.1 reshape.120
  15.0 0.1 mul.72
  15.1 13.3 %cosine_multiply_fusion = (f32[1440,1,512]{2,0,1:T(8,128)S(1)}, f32[1440,1,512]{2,0,1:T(8,128)}) fusion(s32[512]{0:T(512)S(1)} %mul.72), kind=kLoop, calls=%fused_computation.10 | loop fusion | flops 8847360 | bytes 5900288 | tf_op jit(solution)/shard_map/mul | solution.py:16
  28.4 58.1 %all-to-all-done = f32[48,90,256]{2,1,0:T(8,128)} async-done(((f32[48,90,256]{2,1,0:T(8,128)}), f32[48,90,256]{2,1,0:T(8,128)}, u32[]{:S(2)}, u32[]{:S(2)}) %all-to-all-start) | async-done | bytes 4423712 | tf_op jit(solution)/shard_map/all_to_all | solution.py:25
  86.6 5.0 %copy.54 = f32[3,16,90,256]{3,2,1,0:T(8,128)} copy(f32[3,16,90,256]{3,2,0,1:T(8,128)} %bitcast.8) | data formatting | bytes 8847360 | tf_op jit(solution)/shard_map/all_to_all | solution.py:25
  91.6 5.5 %reshape.122 = f32[3,1440,256,1]{2,1,0,3:T(8,128)} reshape(f32[3,16,90,256]{3,2,1,0:T(8,128)} %copy.54) | data formatting | bytes 8847360 | tf_op jit(solution)/shard_map/all_to_all | solution.py:25
  97.1 20.6 %fusion.8 = f32[512,3,2,256]{3,0,1,2:T(8,128)S(1)} fusion(f32[3,1440,256,1]{2,1,0,3:T(8,128)} %reshape.122, f32[1440,1,512]{2,0,1:T(8,128)} %get-tuple-element.10, f32[1440,1,512]{2,0,1:T(8,128)S(1)} %get-tuple-element.9), kind=kOutput, calls=%fused_computation.15 | convolution fusion | flops 13591019520 | bytes 13467648 | tf_op jit(solution)/shard_map/anc,nsk->kasc/dot_general | solution.py:28
  117.8 2.4 copy.55
  120.2 44.2 %all_to_all.54 = f32[512,3,2,256]{3,2,1,0:T(2,128)S(1)} all-to-all(f32[512,3,2,256]{3,2,1,0:T(2,128)S(1)} %copy.55), channel_id=1, replica_groups=mesh['lat'=16,'lon'=16] {'lon'}, dimensions={0} | all-to-all | bytes 6291456 | tf_op jit(solution)/shard_map/all_to_all | solution.py:29
  164.4 0.3 copy.56
  164.7 0.2 copy.57
  165.0 4.1 %copy.58 = f32[32,48,2,256]{3,2,1,0:T(2,128)} copy(f32[32,48,2,256]{3,0,2,1:T(8,128)S(1)} %bitcast.58) | data formatting | bytes 6291456 | tf_op jit(solution)/shard_map/all_to_all | solution.py:29
  169.0 13.9 %all-to-all-start.2 = ((f32[32,48,2,256]{3,2,1,0:T(2,128)}), f32[32,48,2,256]{3,2,1,0:T(2,128)S(1)}, u32[]{:S(2)}, u32[]{:S(2)}) async-start(f32[32,48,2,256]{3,2,1,0:T(2,128)} %copy.58), calls=%async_computation.2 | async-start | bytes 6291456 | tf_op jit(solution)/shard_map/all_to_all | solution.py:30
  182.9 3.6 %reshape.119 = f32[2,384,360,2]{1,3,2,0:T(2,128)} reshape(f32[2,384,720]{1,2,0:T(8,128)} %param.5) | data formatting | bytes 4423680 | tf_op jit(solution)/shard_map/reshape | solution.py:41
  186.5 0.1 fusion.27
  186.6 5.6 %fusion.30 = (f32[2,384,360,1]{1,3,2,0:T(1,128)}, f32[2,384,360,1]{1,3,2,0:T(1,128)}) fusion(f32[2,384,360,2]{1,3,2,0:T(2,128)} %reshape.119), kind=kLoop, calls=%fused_computation.39 | loop fusion | bytes 4423680 | tf_op jit(solution)/shard_map/slice | solution.py:43
  192.2 61.6 %all-to-all-done.2 = f32[32,48,2,256]{3,2,1,0:T(2,128)S(1)} async-done(((f32[32,48,2,256]{3,2,1,0:T(2,128)}), f32[32,48,2,256]{3,2,1,0:T(2,128)S(1)}, u32[]{:S(2)}, u32[]{:S(2)}) %all-to-all-start.2) | async-done | bytes 3145760 | tf_op jit(solution)/shard_map/all_to_all | solution.py:30
  253.8 0.4 copy.59
  254.2 0.3 copy.60
  254.5 1.2 slice.21
  255.7 12.7 %rev.4 = f32[2,384,2,256]{3,1,2,0:T(8,128)} reverse(f32[2,384,2,256]{3,1,2,0:T(8,128)} %slice.21), dimensions={1} | reverse | bytes 3145728 | tf_op jit(solution)/shard_map/jit(_flip)/rev | solution.py:33
  268.4 4.8 %fusion.15 = f32[2,360,1,2,256]{4,1,3,0,2:T(8,128)S(1)} fusion(f32[2,384,2,256]{3,1,2,0:T(8,128)} %rev.4, f32[2,768,2,256]{3,1,2,0:T(8,128)S(1)} %bitcast.55, f32[2,384,360,1]{1,3,2,0:T(1,128)} %get-tuple-element.8, f32[2,384,360,1]{1,3,2,0:T(1,128)} %get-tuple-element.7, pred[2]{0:T(512)(128)(4,1)S(1)} %fusion.27), kind=kOutput, calls=%fused_computation.23 | convolution fusion | flops 1699362816 | bytes 6832640 | tf_op jit(solution)/shard_map/tjk,tjsc->tksc/dot_general | solution.py:45
  273.2 2.6 fusion.18
  275.9 0.4 pad_maximum_fusion.1
  276.3 3.1 %copy.61 = f32[2,360,2,2,256]{4,3,2,1,0:T(2,128)} copy(f32[2,360,2,2,256]{4,1,3,0,2:T(8,128)S(1)} %get-tuple-element.6) | data formatting | bytes 5898240 | tf_op jit(solution)/shard_map/stack | solution.py:49
  279.4 5.5 %stack.27 = f32[2,720,512]{2,1,0:T(8,128)} reshape(f32[2,360,2,2,256]{4,3,2,1,0:T(2,128)} %copy.61) | data formatting | bytes 5898240 | tf_op jit(solution)/shard_map/stack | solution.py:49
  284.9 3.1 %copy.62 = f32[2,360,2,2,256]{4,3,2,1,0:T(2,128)} copy(f32[2,360,2,2,256]{4,1,3,0,2:T(8,128)S(1)} %get-tuple-element.5) | data formatting | bytes 5898240 | tf_op jit(solution)/shard_map/stack | solution.py:49
  288.0 5.4 %stack.29 = f32[2,720,512]{2,1,0:T(8,128)} reshape(f32[2,360,2,2,256]{4,3,2,1,0:T(2,128)} %copy.62) | data formatting | bytes 5898240 | tf_op jit(solution)/shard_map/stack | solution.py:49
  293.4 4.2 %broadcast_select_fusion = f32[2,720,512]{2,1,0:T(8,128)} fusion(f32[2,720,512]{2,1,0:T(8,128)S(1)} %copy-done.1, f32[2,720,512]{2,1,0:T(8,128)} %stack.29, pred[2]{0:T(512)(128)(4,1)S(1)} %fusion.27), kind=kLoop, calls=%fused_computation.22 | loop fusion | flops 737280 | bytes 8847362 | tf_op jit(solution)/shard_map/jit(_where)/select_n | solution.py:48
  (10 shorter events, 0.1 us)
Async XLA Ops:
  7.0 7.8 %copy-start.4 = (s32[512]{0:T(512)S(1)}, s32[512]{0:T(512)}, u32[]{:S(2)}) copy-start(s32[512]{0:T(512)} %param.4) | copy-start | bytes 6148
  7.0 79.6 %all-to-all-start = ((f32[48,90,256]{2,1,0:T(8,128)}), f32[48,90,256]{2,1,0:T(8,128)}, u32[]{:S(2)}, u32[]{:S(2)}) async-start(f32[48,90,256]{2,1,0:T(8,128)} %copy.53), calls=%async_computation | async-start | bytes 9437184 | tf_op jit(solution)/shard_map/all_to_all | solution.py:25
  169.0 84.8 %all-to-all-start.2 = ((f32[32,48,2,256]{3,2,1,0:T(2,128)}), f32[32,48,2,256]{3,2,1,0:T(2,128)S(1)}, u32[]{:S(2)}, u32[]{:S(2)}) async-start(f32[32,48,2,256]{3,2,1,0:T(2,128)} %copy.58), calls=%async_computation.2 | async-start | bytes 6291456 | tf_op jit(solution)/shard_map/all_to_all | solution.py:30
  268.4 4.8 %copy-start = (f32[2,384,2,256]{3,1,2,0:T(8,128)S(1)}, f32[2,384,2,256]{3,1,2,0:T(8,128)}, u32[]{:S(2)}) copy-start(f32[2,384,2,256]{3,1,2,0:T(8,128)} %rev.4) | copy-start | bytes 4718596
  268.4 4.8 %copy-start.2 = (f32[2,384,360,1]{1,3,2,0:T(1,128)S(1)}, f32[2,384,360,1]{1,3,2,0:T(1,128)}, u32[]{:S(2)}) copy-start(f32[2,384,360,1]{1,3,2,0:T(1,128)} %get-tuple-element.7) | copy-start | bytes 3317764
  268.4 4.8 %copy-start.3 = (f32[2,384,360,1]{1,3,2,0:T(1,128)S(1)}, f32[2,384,360,1]{1,3,2,0:T(1,128)}, u32[]{:S(2)}) copy-start(f32[2,384,360,1]{1,3,2,0:T(1,128)} %get-tuple-element.8) | copy-start | bytes 3317764
  288.0 5.4 %copy-start.1 = (f32[2,720,512]{2,1,0:T(8,128)S(1)}, f32[2,720,512]{2,1,0:T(8,128)}, u32[]{:S(2)}) copy-start(f32[2,720,512]{2,1,0:T(8,128)} %stack.27) | copy-start | bytes 8847364
where the time goes:
time: 304 us; the launch traced here: 298 us
  waiting for transfers between devices  120 us (39%)
  local copies, waits for them, and re-layouts  65.8 us (22%)
  blocking collectives  44.2 us (15%)
  matrix products  28.1 us (9%)
  starting transfers between devices  21.7 us (7%)
  other arithmetic  18 us (6%)
    all_to_all x1, waiting for transfers between devices, on_device(): lax.all_to_all(wave_blocks, 'lat', split_axis=0, concat_axis=1, tiled=True)  61.6 us
    all_to_all x1, waiting for transfers between devices, on_device(): lax.all_to_all(grid_values, 'lon', split_axis=0, concat_axis=1, tiled=True)  58.1 us
    all_to_all x1, blocking collectives, on_device(): lax.all_to_all(spectrum, 'lon', split_axis=0, concat_axis=1, tiled=True)  44.2 us
    dot_general x1, matrix products, on_device(): spectrum = jnp.einsum('anc,nsk->kasc', circles, matrix, precision=highest)  20.6 us
    all_to_all x1, starting transfers between devices, on_device(): lax.all_to_all(wave_blocks, 'lat', split_axis=0, concat_axis=1, tiled=True)  13.9 us
    mul x1, other arithmetic, fourier_matrix(): jnp.cos(angles) * factor  13.3 us
    rev x1, local copies, waits for them, and re-layouts, on_device(): southern = jnp.flip(gathered[:, half_rows:], axis=1)  12.7 us
    all_to_all x2, local copies, waits for them, and re-layouts, on_device(): lax.all_to_all(grid_values, 'lon', split_axis=0, concat_axis=1, tiled=True)  10.5 us
  transfers between devices with their start and end apart: 2, of which 2 were waited for; matrix products, arithmetic and copies ran while one was open for 8% of the time, Pallas kernels for 0%

commit v1 on v0

v1 whole, which is shorter than its diff:
```python
import functools
import math

import jax
import jax.numpy as jnp
from jax import lax
from jax.experimental import pallas as pl
from jax.experimental.pallas import tpu as pltpu
from jax.sharding import PartitionSpec as P

CIRCLE = 1440
LANES = 128
SECTORS = 16
BANDS = 16
SECTOR_ROWS = 96
POINTS = SECTORS * SECTOR_ROWS
THIRDS = 3
HALVES = 2
CHUNKS = THIRDS * HALVES
BLOCK = 64
ALL_ROWS = 16 * BLOCK


def split(values):
    high = values.astype(jnp.bfloat16)
    low = (values - high.astype(jnp.float32)).astype(jnp.bfloat16)
    return high, low


def unit_circle(turns):
    half = turns * math.pi
    square = half * half
    sine = jnp.full_like(half, -1.0 / 39916800.0)
    for order in (9, 7, 5, 3, 1):
        sine = sine * square + (-1.0) ** (order // 2) / math.factorial(order)
    sine = sine * half
    cosine = jnp.full_like(half, 1.0 / 479001600.0)
    for order in (10, 8, 6, 4, 2, 0):
        cosine = cosine * square + (-1.0) ** (order // 2) / math.factorial(order)
    return 1.0 - 2.0 * sine * sine, 2.0 * sine * cosine


def fraction(product, circle):
    whole = jnp.floor(product * (1.0 / circle) + 0.5)
    return (product - whole * circle) * (1.0 / circle)


def kernel(
    grid, waves, basis, out,
    circles, matrix_high, matrix_low, points, send_lat, recv_lat, send_lon, recv_lon,
    table, table_high, table_low, total,
    sems, own_sems, local_sems, out_sems,
):
    lat = lax.axis_index("lat")
    lon = lax.axis_index("lon")
    place = jnp.where(lat < 8, lat, 23 - lat)
    basis_copy = pltpu.make_async_copy(basis, table, local_sems.at[0])
    basis_copy.start()

    barrier = pltpu.get_barrier_semaphore()

    def greet(step, _):
        pl.semaphore_signal(barrier, inc=1, device_id={"lon": lax.rem(lon + step, SECTORS)}, device_id_type=pl.DeviceIdType.MESH)
        pl.semaphore_signal(barrier, inc=1, device_id={"lat": lax.rem(lat + step, BANDS)}, device_id_type=pl.DeviceIdType.MESH)
        return 0

    lax.fori_loop(1, 16, greet, 0)
    pl.semaphore_wait(barrier, 30)

    def circle_row(third, owner):
        row = 16 * third + owner
        return jnp.where(lat < 8, row, 47 - row)

    def send_circles(chunk):
        half, third = divmod(chunk, THIRDS)
        lanes = pl.ds(half * LANES, LANES)

        def one(step, _):
            peer = lax.rem(lon + step, SECTORS)
            pltpu.make_async_remote_copy(
                src_ref=grid.at[circle_row(third, peer), :, lanes],
                dst_ref=circles.at[chunk, lon],
                send_sem=sems.at[0, chunk],
                recv_sem=sems.at[1, chunk],
                device_id={"lon": peer},
                device_id_type=pl.DeviceIdType.MESH,
            ).start()
            return 0

        lax.fori_loop(1, SECTORS, one, 0)
        pltpu.make_async_copy(grid.at[circle_row(third, lon), :, lanes], circles.at[chunk, lon], own_sems.at[0, chunk]).start()

    def wait_circles(chunk):
        most = circles.at[chunk, pl.ds(0, SECTORS - 1)]
        pltpu.make_async_copy(most, most, sems.at[1, chunk]).wait()
        one = circles.at[chunk, 0]
        pltpu.make_async_copy(one, one, own_sems.at[0, chunk]).wait()

    def send_blocks(stage, axis, me, my_place, source, target, chunk):
        def one(step, _):
            peer = lax.rem(me + step, 16)
            pltpu.make_async_remote_copy(
                src_ref=source.at[chunk, pl.ds(pl.multiple_of(peer * BLOCK, BLOCK), BLOCK)],
                dst_ref=target.at[chunk, pl.ds(pl.multiple_of(my_place * BLOCK, BLOCK), BLOCK)],
                send_sem=sems.at[2 * stage, chunk],
                recv_sem=sems.at[2 * stage + 1, chunk],
                device_id={axis: peer},
                device_id_type=pl.DeviceIdType.MESH,
            ).start()
            return 0

        lax.fori_loop(1, 16, one, 0)
        pltpu.make_async_copy(
            source.at[chunk, pl.ds(pl.multiple_of(me * BLOCK, BLOCK), BLOCK)],
            target.at[chunk, pl.ds(pl.multiple_of(my_place * BLOCK, BLOCK), BLOCK)],
            own_sems.at[stage, chunk],
        ).start()

    def wait_blocks(stage, target, chunk):
        most = target.at[chunk, pl.ds(0, 15 * BLOCK)]
        pltpu.make_async_copy(most, most, sems.at[2 * stage + 1, chunk]).wait()
        one = target.at[chunk, pl.ds(0, BLOCK)]
        pltpu.make_async_copy(one, one, own_sems.at[stage, chunk]).wait()

    def build_matrix():
        lane = lax.broadcasted_iota(jnp.int32, (32, LANES), 1).astype(jnp.float32)
        factor = 1.0 / math.sqrt(CIRCLE)

        def one(block, _):
            numbers = waves[pl.ds(pl.multiple_of(block * 32, 32), 32), :]
            for group in range(3):
                position = lane + float(LANES * group)
                sector = jnp.floor(position * (1.0 / 96.0) + 0.001)
                point = position - 6.0 * sector
                cosine, sine = unit_circle(fraction(numbers * point, float(CIRCLE)))
                cosine, sine = cosine * factor, sine * factor
                for quarter in range(4):
                    turn = fraction(numbers * float(quarter), 4.0) * 4.0
                    turn_cos = 1.0 - jnp.abs(turn)
                    turn_sin = jnp.where(turn == -2.0, 0.0, turn)
                    real = turn_cos * cosine - turn_sin * sine
                    imaginary = -turn_sin * cosine - turn_cos * sine
                    columns = pl.ds(384 * quarter + LANES * group, LANES)
                    for offset, values in ((0, real), (32, imaginary)):
                        rows = pl.ds(pl.multiple_of(block * BLOCK + offset, 32), 32)
                        matrix_high[rows, columns], matrix_low[rows, columns] = split(values)
            return 0

        lax.fori_loop(0, 16, one, 0)

    def build_table():
        degree = lax.broadcasted_iota(jnp.int32, (8, 720), 1).astype(jnp.float32)
        first = (lat * SECTORS + lon) * 2
        for slot in range(2):
            wave = waves[pl.ds(first + slot, 1), :][:, :1]
            sign = 1.0 - 4.0 * jnp.abs(fraction(degree + wave, 2.0))
            for third in range(THIRDS):
                rows = []
                for circle in range(16):
                    north = jnp.concatenate(
                        [table[slot, pl.ds(48 * band + 16 * third + circle, 1), :] for band in range(8)], 0
                    )
                    rows += [north, north * sign]
                stacked = jnp.concatenate(rows, 0)
                high, low = split(stacked.T)
                table_high[slot, third], table_low[slot, third] = high, low

    def transform(chunk):
        wait_circles(chunk)

        def cut(sector, _):
            values = circles[chunk, sector]
            values = jnp.concatenate([values, jnp.zeros((SECTOR_ROWS - 90, LANES), jnp.float32)], 0)
            high, low = split(values)
            rows = pl.ds(pl.multiple_of(sector * SECTOR_ROWS, SECTOR_ROWS), SECTOR_ROWS)
            points[rows, :LANES], points[rows, LANES:] = high, low
            return 0

        lax.fori_loop(0, SECTORS, cut, 0)

        def rows_of(part, _):
            rows = pl.ds(pl.multiple_of(part * 256, 256), 256)
            both = jnp.dot(matrix_high[rows, :], points[...], preferred_element_type=jnp.float32)
            rest = jnp.dot(matrix_low[rows, :], points[:, :LANES], preferred_element_type=jnp.float32)
            send_lat[chunk, rows, :] = both[:, :LANES] + both[:, LANES:] + rest
            return 0

        lax.fori_loop(0, 4, rows_of, 0)
        send_blocks(1, "lat", lat, place, send_lat, recv_lat, chunk)

    def turn_over(chunk):
        wait_blocks(1, recv_lat, chunk)

        def one(owner, _):
            for slot in range(2):
                for part in range(2):
                    values = recv_lat[chunk, pl.ds(part * 32 + owner * 2 + slot, 16, stride=BLOCK), :]
                    send_lon[chunk, pl.ds(pl.multiple_of(owner * BLOCK + slot * 32 + part * 16, 16), 16), :] = values
            return 0

        lax.fori_loop(0, SECTORS, one, 0)
        send_blocks(2, "lon", lon, lon, send_lon, recv_lon, chunk)

    def sum_up(chunk):
        half, third = divmod(chunk, THIRDS)
        wait_blocks(2, recv_lon, chunk)
        arrived = recv_lon[chunk].reshape(16, 2, 2, 16, LANES)
        for slot in range(2):
            pair = [arrived[:, slot, part].reshape(256, LANES) for part in range(2)]
            high, low = split(jnp.concatenate(pair, 1))
            one_high, one_low = table_high[slot, third], table_low[slot, third]
            sums = jnp.dot(one_high, high, preferred_element_type=jnp.float32)
            sums += jnp.dot(one_high, low, preferred_element_type=jnp.float32)
            sums += jnp.dot(one_low, high, preferred_element_type=jnp.float32)
            if third:
                sums += total[half, slot]
            total[half, slot] = sums
            if third == THIRDS - 1:
                for part in range(2):
                    out_copy(half, slot, part).start()

    def out_copy(half, slot, part):
        return pltpu.make_async_copy(
            total.at[half, slot, :, pl.ds(part * LANES, LANES)],
            out.at[slot, :, pl.ds(part * 256 + half * LANES, LANES)],
            out_sems.at[half, slot, part],
        )

    def wait_sent(stage, source, chunk):
        if stage == 0:
            most = circles.at[chunk, pl.ds(0, SECTORS - 1)]
        else:
            most = source.at[chunk, pl.ds(0, 15 * BLOCK)]
        pltpu.make_async_copy(most, most, sems.at[2 * stage, chunk]).wait()

    send_circles(0)
    send_circles(1)
    build_matrix()
    for step in range(CHUNKS + 2):
        if step < CHUNKS:
            transform(step)
            if step + 2 < CHUNKS:
                send_circles(step + 2)
            wait_sent(0, None, step)
        if step == 0:
            basis_copy.wait()
            build_table()
        if 1 <= step <= CHUNKS:
            turn_over(step - 1)
            wait_sent(1, send_lat, step - 1)
        if step >= 2:
            sum_up(step - 2)
            wait_sent(2, send_lon, step - 2)
    for half in range(HALVES):
        for slot in range(2):
            for part in range(2):
                out_copy(half, slot, part).wait()


def on_device(grid_values, wave_table, legendre_basis):
    waves = jnp.broadcast_to(wave_table.astype(jnp.float32)[:, None], (512, LANES))
    any_space = pl.BlockSpec(memory_space=pl.ANY)
    return pl.pallas_call(
        kernel,
        out_shape=jax.ShapeDtypeStruct((2, 720, 512), jnp.float32),
        in_specs=[any_space, pl.BlockSpec(memory_space=pltpu.VMEM), any_space],
        out_specs=any_space,
        scratch_shapes=[
            pltpu.VMEM((CHUNKS, SECTORS, 90, LANES), jnp.float32),
            pltpu.VMEM((ALL_ROWS, POINTS), jnp.bfloat16),
            pltpu.VMEM((ALL_ROWS, POINTS), jnp.bfloat16),
            pltpu.VMEM((POINTS, 2 * LANES), jnp.bfloat16),
            pltpu.VMEM((CHUNKS, ALL_ROWS, LANES), jnp.float32),
            pltpu.VMEM((CHUNKS, ALL_ROWS, LANES), jnp.float32),
            pltpu.VMEM((CHUNKS, ALL_ROWS, LANES), jnp.float32),
            pltpu.VMEM((CHUNKS, ALL_ROWS, LANES), jnp.float32),
            pltpu.VMEM((2, 384, 720), jnp.float32),
            pltpu.VMEM((2, THIRDS, 720, 256), jnp.bfloat16),
            pltpu.VMEM((2, THIRDS, 720, 256), jnp.bfloat16),
            pltpu.VMEM((HALVES, 2, 720, 256), jnp.float32),
            pltpu.SemaphoreType.DMA((6, CHUNKS)),
            pltpu.SemaphoreType.DMA((3, CHUNKS)),
            pltpu.SemaphoreType.DMA((2,)),
            pltpu.SemaphoreType.DMA((HALVES, 2, 2)),
        ],
        compiler_params=pltpu.CompilerParams(
            collective_id=0, has_side_effects=True, vmem_limit_bytes=56 * 1024 * 1024
        ),
        name="transform",
    )(grid_values, waves, legendre_basis)


def solution(mesh):
    placed = (P("lat", "lon", None), P(), P(("lat", "lon"), None, None))
    return jax.shard_map(
        on_device,
        mesh=mesh,
        in_specs=placed,
        out_specs=P(("lat", "lon"), None, None),
        check_vma=False,
    )
```

time: 304 us -> 148 us (0.49); the launches traced: 298 us -> 148 us
  Pallas kernels: 0 us -> 133 us
  waiting for transfers between devices: 120 us -> 0 us
  local copies, waits for them, and re-layouts: 65.8 us -> 14.5 us
  blocking collectives: 44.2 us -> 0 us
  matrix products: 28.1 us -> 0 us
  starting transfers between devices: 21.7 us -> 0 us
  other arithmetic: 18 us -> 0.68 us
    pallas_call x0 -> x1, Pallas kernels: none -> 133 us  [on_device(): pl.pallas_call(kernel, out_shape=jax.ShapeDtypeStruct((2, 720, 512), jnp....]
    all_to_all x2 -> x0, waiting for transfers between devices: 120 us -> none  [the longest x1 61.6 us: on_device(): lax.all_to_all(wave_blocks, 'lat', split_axis=0, concat_axis=1, tiled=True)]
    all_to_all x1 -> x0, blocking collectives: 44.2 us -> none  [on_device(): lax.all_to_all(spectrum, 'lon', split_axis=0, concat_axis=1, tiled=True)]
    dot_general x3 -> x0, matrix products: 28.1 us -> none  [the longest x1 20.6 us: on_device(): spectrum = jnp.einsum('anc,nsk->kasc', circles, matrix, precision=highest)]
    all_to_all x2 -> x0, starting transfers between devices: 21.7 us -> none  [the longest x1 13.9 us: on_device(): lax.all_to_all(wave_blocks, 'lat', split_axis=0, concat_axis=1, tiled=True)]
    another operation x4 -> x0, local copies, waits for them, and re-layouts: 17.1 us -> none  [the longest x2 8.57 us: on_device(): jnp.stack([same_sums, other_sums], 2)]
    all_to_all x7 -> x0, local copies, waits for them, and re-layouts: 15.8 us -> none  [the longest x2 10.5 us: on_device(): lax.all_to_all(grid_values, 'lon', split_axis=0, concat_axis=1, tiled=True)]
    mul x1 -> x0, other arithmetic: 13.3 us -> none  [fourier_matrix(): jnp.cos(angles) * factor]
  transfers between devices with their start and end apart: 2 -> 0, of which waited for: 2 -> 0; matrix products, arithmetic and copies ran while one was open for 8% -> 0% of each run, Pallas kernels for 0% -> 0%
where the time goes in v1:
time: 148 us
  Pallas kernels  133 us (90%)
  local copies, waits for them, and re-layouts  14.5 us (10%)
    pallas_call x1, Pallas kernels, on_device(): pl.pallas_call(kernel, out_shape=jax.ShapeDtypeStruct((2, 720, 512), jnp....  133 us
    unnamed x3, local copies, waits for them, and re-layouts  13.7 us

profile of v1, /device:TPU:1, one launch (start us, length us, event | category | flops | bytes accessed | tf_op | source)
XLA Modules:
  0.0 148.1 jit_solution(4015675113418975546)
XLA Ops:
  0.0 0.7 convert_element_type.3
  0.7 0.8 broadcast_in_dim.2.waves
  1.5 3.0 %copy.5.basis = f32[2,384,720]{2,1,0:T(8,128)} copy(f32[2,384,720]{1,2,0:T(8,128)} %param.5) | data formatting | bytes 4423680 | tf_op args[2]
  4.5 7.0 %copy.4.grid = f32[48,90,256]{2,1,0:T(8,128)} copy(f32[48,90,256]{2,0,1:T(8,128)} %param.3) | data formatting | bytes 8847360 | tf_op args[0]
  11.5 132.9 %transform.1 = f32[2,720,512]{2,1,0:T(8,128)} custom-call(f32[48,90,256]{2,1,0:T(8,128)} %copy.4.grid, f32[512,128]{1,0:T(8,128)} %broadcast_in_dim.2.waves, f32[2,384,720]{2,1,0:T(8,128)} %copy.5.basis), custom_call_target="tpu_custom_call" | custom-call | tf_op jit(solution)/shard_map/transform/pallas_call | solution.py:263
  144.4 3.7 %copy.7 = f32[2,720,512]{2,1,0:T(8,128)} copy(f32[2,720,512]{2,1,0:T(8,128)} %transform.1) | data formatting | bytes 5898240

commit v2 on v1

v2 whole, which is shorter than its diff:
```python
import functools
import math

import jax
import jax.numpy as jnp
from jax import lax
from jax.experimental import pallas as pl
from jax.experimental.pallas import tpu as pltpu
from jax.sharding import PartitionSpec as P

CIRCLE = 1440
LANES = 128
SECTORS = 16
BANDS = 16
SECTOR_ROWS = 96
POINTS = SECTORS * SECTOR_ROWS
THIRDS = 3
HALVES = 2
CHUNKS = THIRDS * HALVES
BLOCK = 64
ALL_ROWS = 16 * BLOCK


LON_STEPS = (
    (1, 0), (0, 1), (3, 0), (0, 3), (2, 1), (1, 2), (2, 3), (3, 2), (1, 1), (3, 3), (1, 3), (3, 1), (2, 0), (0, 2), (2, 2),
)
LAT_STEPS = (
    (1, 0), (7, 1), (2, 0), (6, 1), (3, 0), (5, 1), (4, 0), (4, 1), (7, 0), (1, 1), (6, 0), (2, 1), (5, 0), (3, 1), (0, 1),
)


def split(values):
    high = values.astype(jnp.bfloat16)
    low = (values - high.astype(jnp.float32)).astype(jnp.bfloat16)
    return high, low


def unit_circle(turns):
    half = turns * math.pi
    square = half * half
    sine = jnp.full_like(half, -1.0 / 39916800.0)
    for order in (9, 7, 5, 3, 1):
        sine = sine * square + (-1.0) ** (order // 2) / math.factorial(order)
    sine = sine * half
    cosine = jnp.full_like(half, 1.0 / 479001600.0)
    for order in (10, 8, 6, 4, 2, 0):
        cosine = cosine * square + (-1.0) ** (order // 2) / math.factorial(order)
    return 1.0 - 2.0 * sine * sine, 2.0 * sine * cosine


def fraction(product, circle):
    whole = jnp.floor(product * (1.0 / circle) + 0.5)
    return (product - whole * circle) * (1.0 / circle)


def kernel(
    grid, numbers, basis, out,
    rows_held, circles_out, circles, waves, matrix_high, matrix_low, points,
    send_lat, recv_lat, send_lon, recv_lon,
    table, table_high, table_low,
    sems, own_sems, row_sems, table_sem,
):
    lat = lax.axis_index("lat")
    lon = lax.axis_index("lon")
    northern = lat < 8
    place = jnp.where(northern, lat, 23 - lat)

    core = lax.rem(lat, 2)
    turn = 1 - 2 * core

    def lon_peer(step, way):
        x = lax.rem(lon // 4 + way * turn * step[0] + 4, 4)
        y = lax.rem(lax.rem(lon, 4) + way * turn * step[1] + 4, 4)
        return x * 4 + y

    def lat_peer(step):
        z = lax.rem(lat // 2 + turn * step[0] + 8, 8)
        return z * 2 + lax.rem(core + step[1], 2)

    def load_rows(chunk):
        half, third = divmod(chunk, THIRDS)
        first = pl.multiple_of(jnp.where(northern, 16 * third, 32 - 16 * third), 16)
        return pltpu.make_async_copy(
            grid.at[:, pl.ds(first, 16), pl.ds(half * LANES, LANES)], rows_held.at[chunk], row_sems.at[chunk]
        )

    for chunk in range(CHUNKS):
        load_rows(chunk).start()
    table_copy = pltpu.make_async_copy(basis, table, table_sem)
    table_copy.start()

    barrier = pltpu.get_barrier_semaphore()

    def greet(step, _):
        pl.semaphore_signal(barrier, inc=1, device_id={"lon": lax.rem(lon + step, SECTORS)}, device_id_type=pl.DeviceIdType.MESH)
        pl.semaphore_signal(barrier, inc=1, device_id={"lat": lax.rem(lat + step, BANDS)}, device_id_type=pl.DeviceIdType.MESH)
        return 0

    lax.fori_loop(1, 16, greet, 0)

    def arrange(chunk, owner):
        start = jnp.where(northern, owner, 15 - owner)
        circles_out[chunk, owner] = rows_held.at[chunk].reshape(90 * 16, LANES)[pl.ds(start, 90, stride=16), :]

    def send_circle(chunk, peer):
        arrange(chunk, peer)
        pltpu.make_async_remote_copy(
            src_ref=circles_out.at[chunk, peer],
            dst_ref=circles.at[chunk, lon],
            send_sem=sems.at[0, chunk],
            recv_sem=sems.at[1, chunk],
            device_id={"lon": peer},
            device_id_type=pl.DeviceIdType.MESH,
        ).start()

    def keep_circle(chunk):
        arrange(chunk, lon)
        pltpu.make_async_copy(circles_out.at[chunk, lon], circles.at[chunk, lon], own_sems.at[0, chunk]).start()

    def wait_circles(chunk):
        most = circles.at[chunk, pl.ds(0, SECTORS - 1)]
        pltpu.make_async_copy(most, most, sems.at[1, chunk]).wait()
        one = circles.at[chunk, 0]
        pltpu.make_async_copy(one, one, own_sems.at[0, chunk]).wait()

    def block_copy(stage, peer, chunk):
        source, target = ((send_lat, recv_lat), (send_lon, recv_lon))[stage - 1]
        mine = (place, lon)[stage - 1]
        return (
            source.at[chunk, pl.ds(pl.multiple_of(peer * BLOCK, BLOCK), BLOCK)],
            target.at[chunk, pl.ds(pl.multiple_of(mine * BLOCK, BLOCK), BLOCK)],
        )

    def send_block(stage, peer, chunk):
        source, target = block_copy(stage, peer, chunk)
        pltpu.make_async_remote_copy(
            src_ref=source,
            dst_ref=target,
            send_sem=sems.at[2 * stage, chunk],
            recv_sem=sems.at[2 * stage + 1, chunk],
            device_id={("lat", "lon")[stage - 1]: peer},
            device_id_type=pl.DeviceIdType.MESH,
        ).start()

    def keep_block(stage, chunk):
        source, target = block_copy(stage, (lat, lon)[stage - 1], chunk)
        pltpu.make_async_copy(source, target, own_sems.at[stage, chunk]).start()

    def burst(circle_chunk=None, lat_chunk=None, lon_chunk=None):
        if circle_chunk:
            load_rows(circle_chunk).wait()
        for step in range(15):
            if lat_chunk is not None:
                send_block(1, lat_peer(LAT_STEPS[step]), lat_chunk)
            if circle_chunk is not None:
                send_circle(circle_chunk, lon_peer(LON_STEPS[step], 1))
            if lon_chunk is not None:
                send_block(2, lon_peer(LON_STEPS[step], -1), lon_chunk)
        if lat_chunk is not None:
            keep_block(1, lat_chunk)
        if circle_chunk is not None:
            keep_circle(circle_chunk)
        if lon_chunk is not None:
            keep_block(2, lon_chunk)

    def wait_blocks(stage, target, chunk):
        most = target.at[chunk, pl.ds(0, 15 * BLOCK)]
        pltpu.make_async_copy(most, most, sems.at[2 * stage + 1, chunk]).wait()
        one = target.at[chunk, pl.ds(0, BLOCK)]
        pltpu.make_async_copy(one, one, own_sems.at[stage, chunk]).wait()

    def spread_waves():
        for group in range(4):
            values = jnp.broadcast_to(numbers[group : group + 1, :].astype(jnp.float32), (LANES, LANES))
            waves[LANES * group : LANES * (group + 1), :] = values.T

    def build_matrix():
        lane = lax.broadcasted_iota(jnp.int32, (32, LANES), 1).astype(jnp.float32)
        factor = 1.0 / math.sqrt(CIRCLE)

        def one(block, _):
            wave = waves[pl.ds(pl.multiple_of(block * 32, 32), 32), :]
            for group in range(3):
                position = lane + float(LANES * group)
                sector = jnp.floor(position * (1.0 / 96.0) + 0.001)
                point = position - 6.0 * sector
                cosine, sine = unit_circle(fraction(wave * point, float(CIRCLE)))
                cosine, sine = cosine * factor, sine * factor
                for quarter in range(4):
                    turn = fraction(wave * float(quarter), 4.0) * 4.0
                    turn_cos = 1.0 - jnp.abs(turn)
                    turn_sin = jnp.where(turn == -2.0, 0.0, turn)
                    real = turn_cos * cosine - turn_sin * sine
                    imaginary = -turn_sin * cosine - turn_cos * sine
                    columns = pl.ds(384 * quarter + LANES * group, LANES)
                    for offset, values in ((0, real), (32, imaginary)):
                        rows = pl.ds(pl.multiple_of(block * BLOCK + offset, 32), 32)
                        matrix_high[rows, columns], matrix_low[rows, columns] = split(values)
            return 0

        lax.fori_loop(0, 16, one, 0)

    def build_table():
        table_copy.wait()
        degree = lax.broadcasted_iota(jnp.int32, (720, 256), 0).astype(jnp.float32)
        southern = (lax.broadcasted_iota(jnp.int32, (720, 256), 1) & 8) == 8
        row = lax.broadcasted_iota(jnp.int32, (384, 256), 0)
        column = lax.broadcasted_iota(jnp.int32, (384, 256), 1)
        wanted = 48 * (column & 7) + (column >> 4)
        first = (lat * SECTORS + lon) * 2
        for slot in range(2):
            wave = jnp.broadcast_to(waves[pl.ds(first + slot, 1), :][:, :1], (1, 256))
            sign = 1.0 - 4.0 * jnp.abs(fraction(degree + wave, 2.0))
            sign = jnp.where(southern, sign, 1.0)
            parts = split(table[slot])
            for third in range(THIRDS):
                pick = jnp.where(row == wanted + 16 * third, 1.0, 0.0).astype(jnp.bfloat16)
                for part, target in zip(parts, (table_high, table_low)):
                    placed = jnp.dot(part, pick, preferred_element_type=jnp.float32)
                    target[slot, third] = (placed * sign).astype(jnp.bfloat16)

    def transform(chunk):
        wait_circles(chunk)

        def cut(sector, _):
            values = circles[chunk, sector]
            values = jnp.concatenate([values, jnp.zeros((SECTOR_ROWS - 90, LANES), jnp.float32)], 0)
            high, low = split(values)
            rows = pl.ds(pl.multiple_of(sector * SECTOR_ROWS, SECTOR_ROWS), SECTOR_ROWS)
            points[rows, :LANES], points[rows, LANES:] = high, low
            return 0

        lax.fori_loop(0, SECTORS, cut, 0)

        def rows_of(part, _):
            rows = pl.ds(pl.multiple_of(part * 256, 256), 256)
            both = jnp.dot(matrix_high[rows, :], points[...], preferred_element_type=jnp.float32)
            rest = jnp.dot(matrix_low[rows, :], points[:, :LANES], preferred_element_type=jnp.float32)
            send_lat[chunk, rows, :] = both[:, :LANES] + both[:, LANES:] + rest
            return 0

        lax.fori_loop(0, 4, rows_of, 0)

    def turn_over(chunk):
        wait_blocks(1, recv_lat, chunk)

        def one(owner, _):
            for slot in range(2):
                for part in range(2):
                    values = recv_lat[chunk, pl.ds(part * 32 + owner * 2 + slot, 16, stride=BLOCK), :]
                    send_lon[chunk, pl.ds(pl.multiple_of(owner * BLOCK + slot * 32 + part * 16, 16), 16), :] = values
            return 0

        lax.fori_loop(0, SECTORS, one, 0)

    def sum_up(chunk):
        half, third = divmod(chunk, THIRDS)
        wait_blocks(2, recv_lon, chunk)
        arrived = recv_lon[chunk].reshape(16, 2, 2, 16, LANES)
        for slot in range(2):
            pair = [arrived[:, slot, part].reshape(256, LANES) for part in range(2)]
            high, low = split(jnp.concatenate(pair, 1))
            one_high, one_low = table_high[slot, third], table_low[slot, third]
            sums = jnp.dot(one_high, high, preferred_element_type=jnp.float32)
            sums += jnp.dot(one_high, low, preferred_element_type=jnp.float32)
            sums += jnp.dot(one_low, high, preferred_element_type=jnp.float32)
            for part in range(2):
                columns = pl.ds(part * 256 + half * LANES, LANES)
                piece = sums[:, part * LANES : (part + 1) * LANES]
                out[slot, :, columns] = out[slot, :, columns] + piece if third else piece

    def wait_sent(stage, source, chunk):
        if stage == 0:
            most = circles.at[chunk, pl.ds(0, SECTORS - 1)]
        else:
            most = source.at[chunk, pl.ds(0, 15 * BLOCK)]
        pltpu.make_async_copy(most, most, sems.at[2 * stage, chunk]).wait()

    load_rows(0).wait()
    pl.semaphore_wait(barrier, 30)
    burst(0)
    spread_waves()
    build_matrix()
    burst(1)
    transform(0)
    burst(2, 0)
    build_table()
    transform(1)
    burst(3, 1)
    turn_over(0)
    transform(2)
    burst(4, 2, 0)
    turn_over(1)
    transform(3)
    burst(5, 3, 1)
    turn_over(2)
    transform(4)
    burst(None, 4, 2)
    sum_up(0)
    turn_over(3)
    transform(5)
    burst(None, 5, 3)
    sum_up(1)
    turn_over(4)
    burst(None, None, 4)
    sum_up(2)
    sum_up(3)
    turn_over(5)
    burst(None, None, 5)
    sum_up(4)
    sum_up(5)
    for chunk in range(CHUNKS):
        wait_sent(0, None, chunk)
        wait_sent(1, send_lat, chunk)
        wait_sent(2, send_lon, chunk)


def on_device(grid_values, wave_table, legendre_basis):
    any_space = pl.BlockSpec(memory_space=pl.ANY)
    vmem = pl.BlockSpec(memory_space=pltpu.VMEM)
    return pl.pallas_call(
        kernel,
        out_shape=pltpu.VMEM((2, 720, 512), jnp.float32),
        in_specs=[any_space, vmem, any_space],
        out_specs=vmem,
        scratch_shapes=[
            pltpu.VMEM((CHUNKS, 90, 16, LANES), jnp.float32),
            pltpu.VMEM((CHUNKS, SECTORS, 90, LANES), jnp.float32),
            pltpu.VMEM((CHUNKS, SECTORS, 90, LANES), jnp.float32),
            pltpu.VMEM((512, LANES), jnp.float32),
            pltpu.VMEM((ALL_ROWS, POINTS), jnp.bfloat16),
            pltpu.VMEM((ALL_ROWS, POINTS), jnp.bfloat16),
            pltpu.VMEM((POINTS, 2 * LANES), jnp.bfloat16),
            pltpu.VMEM((CHUNKS, ALL_ROWS, LANES), jnp.float32),
            pltpu.VMEM((CHUNKS, ALL_ROWS, LANES), jnp.float32),
            pltpu.VMEM((CHUNKS, ALL_ROWS, LANES), jnp.float32),
            pltpu.VMEM((CHUNKS, ALL_ROWS, LANES), jnp.float32),
            pltpu.VMEM((2, 720, 384), jnp.float32),
            pltpu.VMEM((2, THIRDS, 720, 256), jnp.bfloat16),
            pltpu.VMEM((2, THIRDS, 720, 256), jnp.bfloat16),
            pltpu.SemaphoreType.DMA((6, CHUNKS)),
            pltpu.SemaphoreType.DMA((3, CHUNKS)),
            pltpu.SemaphoreType.DMA((CHUNKS,)),
            pltpu.SemaphoreType.DMA,
        ],
        compiler_params=pltpu.CompilerParams(
            collective_id=0, has_side_effects=True, vmem_limit_bytes=56 * 1024 * 1024
        ),
        name="transform",
    )(jnp.swapaxes(grid_values, 0, 1), wave_table.reshape(4, LANES), jnp.swapaxes(legendre_basis, 1, 2))


def solution(mesh):
    placed = (P("lat", "lon", None), P(), P(("lat", "lon"), None, None))
    return jax.shard_map(
        on_device,
        mesh=mesh,
        in_specs=placed,
        out_specs=P(("lat", "lon"), None, None),
        check_vma=False,
    )
```

time: 148 us -> 106 us (0.72)
  Pallas kernels: 133 us -> 104 us
  local copies, waits for them, and re-layouts: 14.5 us -> 1.6 us
    pallas_call x1, Pallas kernels: 133 us -> 104 us  [on_device(): pl.pallas_call(kernel, out_shape=pltpu.VMEM((2, 720, 512), jnp.float32),...]
    unnamed x3 -> x1, local copies, waits for them, and re-layouts: 13.7 us -> 1.6 us
where the time goes in v2:
time: 106 us; the launch traced here: 105 us
  Pallas kernels  104 us (98%)
  local copies, waits for them, and re-layouts  1.6 us (2%)
    pallas_call x1, Pallas kernels, on_device(): pl.pallas_call(kernel, out_shape=pltpu.VMEM((2, 720, 512), jnp.float32),...  104 us

profile of v2, /device:TPU:1, one launch (start us, length us, event | category | flops | bytes accessed | tf_op | source)
XLA Modules:
  0.0 105.4 jit_solution(17471672451724052969)
XLA Ops:
  0.0 103.8 %transform.1 = f32[2,720,512]{2,1,0:T(8,128)S(1)} custom-call(f32[90,48,256]{2,1,0:T(8,128)} %bitcast.3, s32[4,128]{1,0:T(4,128)} %bitcast.5, f32[2,720,384]{2,1,0:T(8,128)} %bitcast.4), custom_call_target="tpu_custom_call" | custom-call | tf_op jit(solution)/shard_map/transform/pallas_call | solution.py:321
  103.8 1.6 %copy.5 = f32[2,720,512]{2,1,0:T(8,128)} copy(f32[2,720,512]{2,1,0:T(8,128)S(1)} %transform.1) | data formatting | bytes 5898240

commit v3 on v2

--- a/solution.py
+++ b/solution.py
@@ -103,7 +103,8 @@
         circles_out[chunk, owner] = rows_held.at[chunk].reshape(90 * 16, LANES)[pl.ds(start, 90, stride=16), :]
 
     def send_circle(chunk, peer):
-        arrange(chunk, peer)
+        if chunk:
+            arrange(chunk, peer)
         pltpu.make_async_remote_copy(
             src_ref=circles_out.at[chunk, peer],
             dst_ref=circles.at[chunk, lon],
@@ -114,7 +115,8 @@
         ).start()
 
     def keep_circle(chunk):
-        arrange(chunk, lon)
+        if chunk:
+            arrange(chunk, lon)
         pltpu.make_async_copy(circles_out.at[chunk, lon], circles.at[chunk, lon], own_sems.at[0, chunk]).start()
 
     def wait_circles(chunk):
@@ -146,22 +148,19 @@
         source, target = block_copy(stage, (lat, lon)[stage - 1], chunk)
         pltpu.make_async_copy(source, target, own_sems.at[stage, chunk]).start()
 
-    def burst(circle_chunk=None, lat_chunk=None, lon_chunk=None):
-        if circle_chunk:
-            load_rows(circle_chunk).wait()
-        for step in range(15):
-            if lat_chunk is not None:
-                send_block(1, lat_peer(LAT_STEPS[step]), lat_chunk)
-            if circle_chunk is not None:
-                send_circle(circle_chunk, lon_peer(LON_STEPS[step], 1))
-            if lon_chunk is not None:
-                send_block(2, lon_peer(LON_STEPS[step], -1), lon_chunk)
-        if lat_chunk is not None:
-            keep_block(1, lat_chunk)
-        if circle_chunk is not None:
-            keep_circle(circle_chunk)
-        if lon_chunk is not None:
-            keep_block(2, lon_chunk)
+    def circle_messages(chunk):
+        return [functools.partial(lambda step: send_circle(chunk, lon_peer(step, 1)), step) for step in LON_STEPS]
+
+    def lat_messages(chunk):
+        return [functools.partial(lambda step: send_block(1, lat_peer(step), chunk), step) for step in LAT_STEPS]
+
+    def lon_messages(chunk):
+        return [functools.partial(lambda step: send_block(2, lon_peer(step, -1), chunk), step) for step in LON_STEPS]
+
+    def burst(*lists):
+        order = [((place + 0.5) / len(each), index, message) for index, each in enumerate(lists) for place, message in enumerate(each)]
+        for _, _, message in sorted(order, key=lambda entry: entry[:2]):
+            message()
 
     def wait_blocks(stage, target, chunk):
         most = target.at[chunk, pl.ds(0, 15 * BLOCK)]
@@ -203,21 +202,26 @@
     def build_table():
         table_copy.wait()
         degree = lax.broadcasted_iota(jnp.int32, (720, 256), 0).astype(jnp.float32)
-        southern = (lax.broadcasted_iota(jnp.int32, (720, 256), 1) & 8) == 8
         row = lax.broadcasted_iota(jnp.int32, (384, 256), 0)
         column = lax.broadcasted_iota(jnp.int32, (384, 256), 1)
-        wanted = 48 * (column & 7) + (column >> 4)
+        wide_column = lax.broadcasted_iota(jnp.int32, (720, 256), 1)
         first = (lat * SECTORS + lon) * 2
         for slot in range(2):
             wave = jnp.broadcast_to(waves[pl.ds(first + slot, 1), :][:, :1], (1, 256))
             sign = 1.0 - 4.0 * jnp.abs(fraction(degree + wave, 2.0))
-            sign = jnp.where(southern, sign, 1.0)
             parts = split(table[slot])
-            for third in range(THIRDS):
-                pick = jnp.where(row == wanted + 16 * third, 1.0, 0.0).astype(jnp.bfloat16)
+            for kind in range(THIRDS + 1):
+                if kind < THIRDS:
+                    wanted = 48 * (column & 7) + (column >> 4) + 16 * kind
+                    southern = (wide_column & 8) == 8
+                else:
+                    wanted = 48 * ((column >> 4) & 7) + (column & 15) + 16 * (THIRDS - 1)
+                    southern = wide_column >= 128
+                pick = jnp.where(row == wanted, 1.0, 0.0).astype(jnp.bfloat16)
+                signs = jnp.where(southern, sign, 1.0)
                 for part, target in zip(parts, (table_high, table_low)):
                     placed = jnp.dot(part, pick, preferred_element_type=jnp.float32)
-                    target[slot, third] = (placed * sign).astype(jnp.bfloat16)
+                    target[slot, kind] = (placed * signs).astype(jnp.bfloat16)
 
     def transform(chunk):
         wait_circles(chunk)
@@ -232,14 +236,50 @@
 
         lax.fori_loop(0, SECTORS, cut, 0)
 
-        def rows_of(part, _):
+        def rows_of(part):
             rows = pl.ds(pl.multiple_of(part * 256, 256), 256)
             both = jnp.dot(matrix_high[rows, :], points[...], preferred_element_type=jnp.float32)
             rest = jnp.dot(matrix_low[rows, :], points[:, :LANES], preferred_element_type=jnp.float32)
             send_lat[chunk, rows, :] = both[:, :LANES] + both[:, LANES:] + rest
-            return 0
-
-        lax.fori_loop(0, 4, rows_of, 0)
+
+        if chunk:
+            lax.fori_loop(0, 4, lambda part, _: (rows_of(part), 0)[1], 0)
+            return
+        mine = lat // 4
+
+        def one(step, _):
+            part = lax.rem(mine + turn * (1 + 2 * step - 3 * (step // 2)) + 4, 4)
+            rows_of(part)
+            for number in range(4):
+                send_block(1, part * 4 + lax.rem(lat + number, 4), 0)
+            return 0
+
+        lax.fori_loop(0, 3, one, 0)
+        rows_of(mine)
+        for number in range(1, 4):
+            send_block(1, mine * 4 + lax.rem(lat + number, 4), 0)
+        keep_block(1, 0)
+
+    def regroup(chunk):
+        def one(owner, _):
+            for slot in range(2):
+                values = send_lat[chunk, pl.ds(owner * 2 + slot, 32, stride=32), :]
+                send_lon[chunk, pl.ds(pl.multiple_of(owner * BLOCK + slot * 32, 32), 32), :] = values
+            return 0
+
+        lax.fori_loop(0, SECTORS, one, 0)
+
+    def turn_late(chunk):
+        wait_blocks(2, recv_lon, chunk)
+
+        def one(owner, _):
+            for slot in range(2):
+                for part in range(2):
+                    values = recv_lon[chunk, pl.ds(slot * 32 + owner * 2 + part, 16, stride=BLOCK), :]
+                    send_lat[chunk, pl.ds(pl.multiple_of(owner * BLOCK + slot * 32 + part * 16, 16), 16), :] = values
+            return 0
+
+        lax.fori_loop(0, BANDS, one, 0)
 
     def turn_over(chunk):
         wait_blocks(1, recv_lat, chunk)
@@ -255,12 +295,17 @@
 
     def sum_up(chunk):
         half, third = divmod(chunk, THIRDS)
-        wait_blocks(2, recv_lon, chunk)
-        arrived = recv_lon[chunk].reshape(16, 2, 2, 16, LANES)
+        late = chunk == CHUNKS - 1
+        if late:
+            wait_blocks(1, recv_lat, chunk)
+        else:
+            wait_blocks(2, recv_lon, chunk)
+        arrived = (recv_lat if late else recv_lon)[chunk].reshape(16, 2, 2, 16, LANES)
         for slot in range(2):
             pair = [arrived[:, slot, part].reshape(256, LANES) for part in range(2)]
             high, low = split(jnp.concatenate(pair, 1))
-            one_high, one_low = table_high[slot, third], table_low[slot, third]
+            kind = THIRDS if late else third
+            one_high, one_low = table_high[slot, kind], table_low[slot, kind]
             sums = jnp.dot(one_high, high, preferred_element_type=jnp.float32)
             sums += jnp.dot(one_high, low, preferred_element_type=jnp.float32)
             sums += jnp.dot(one_low, high, preferred_element_type=jnp.float32)
@@ -277,36 +322,57 @@
         pltpu.make_async_copy(most, most, sems.at[2 * stage, chunk]).wait()
 
     load_rows(0).wait()
+    lax.fori_loop(0, SECTORS, lambda owner, _: (arrange(0, owner), 0)[1], 0)
     pl.semaphore_wait(barrier, 30)
-    burst(0)
+    burst(circle_messages(0))
+    keep_circle(0)
     spread_waves()
     build_matrix()
-    burst(1)
+    for chunk in range(1, CHUNKS):
+        load_rows(chunk).wait()
+    burst(circle_messages(1))
+    keep_circle(1)
     transform(0)
-    burst(2, 0)
+    burst(circle_messages(2))
+    keep_circle(2)
     build_table()
     transform(1)
-    burst(3, 1)
+    burst(lat_messages(1), circle_messages(3), circle_messages(4)[:8])
+    keep_block(1, 1)
+    keep_circle(3)
+    transform(2)
+    burst(lat_messages(2), circle_messages(4)[8:] + circle_messages(5))
+    keep_block(1, 2)
+    keep_circle(4)
+    keep_circle(5)
+    transform(3)
     turn_over(0)
-    transform(2)
-    burst(4, 2, 0)
+    burst(lat_messages(3), lon_messages(0))
+    keep_block(1, 3)
+    keep_block(2, 0)
+    transform(4)
+    transform(5)
+    regroup(5)
+    burst(lon_messages(5))
+    keep_block(2, 5)
     turn_over(1)
-    transform(3)
-    burst(5, 3, 1)
     turn_over(2)
-    transform(4)
-    burst(None, 4, 2)
+    burst(lat_messages(4), lon_messages(1) + lon_messages(2))
+    keep_block(1, 4)
+    keep_block(2, 1)
+    keep_block(2, 2)
     sum_up(0)
+    turn_late(5)
     turn_over(3)
-    transform(5)
-    burst(None, 5, 3)
+    burst(lat_messages(5), lon_messages(3))
+    keep_block(1, 5)
+    keep_block(2, 3)
     sum_up(1)
+    sum_up(2)
     turn_over(4)
-    burst(None, None, 4)
-    sum_up(2)
+    burst(lon_messages(4))
+    keep_block(2, 4)
     sum_up(3)
-    turn_over(5)
-    burst(None, None, 5)
     sum_up(4)
     sum_up(5)
     for chunk in range(CHUNKS):
@@ -336,8 +402,8 @@
             pltpu.VMEM((CHUNKS, ALL_ROWS, LANES), jnp.float32),
             pltpu.VMEM((CHUNKS, ALL_ROWS, LANES), jnp.float32),
             pltpu.VMEM((2, 720, 384), jnp.float32),
-            pltpu.VMEM((2, THIRDS, 720, 256), jnp.bfloat16),
-            pltpu.VMEM((2, THIRDS, 720, 256), jnp.bfloat16),
+            pltpu.VMEM((2, THIRDS + 1, 720, 256), jnp.bfloat16),
+            pltpu.VMEM((2, THIRDS + 1, 720, 256), jnp.bfloat16),
             pltpu.SemaphoreType.DMA((6, CHUNKS)),
             pltpu.SemaphoreType.DMA((3, CHUNKS)),
             pltpu.SemaphoreType.DMA((CHUNKS,)),

time: 106 us -> 99.2 us (0.936)
  Pallas kernels: 104 us -> 96 us
    pallas_call x1, Pallas kernels: 104 us -> 96 us  [on_device(): pl.pallas_call(kernel, out_shape=pltpu.VMEM((2, 720, 512), jnp.float32),...]
where the time goes in v3:
time: 99.2 us; the launch traced here: 97.6 us
  Pallas kernels  96 us (97%)
  local copies, waits for them, and re-layouts  1.6 us (2%)
    pallas_call x1, Pallas kernels, on_device(): pl.pallas_call(kernel, out_shape=pltpu.VMEM((2, 720, 512), jnp.float32),...  96 us

profile of v3, /device:TPU:1, one launch (start us, length us, event | category | flops | bytes accessed | tf_op | source)
XLA Modules:
  0.0 97.6 jit_solution(11229768827808986609)
XLA Ops:
  0.0 96.0 %transform.1 = f32[2,720,512]{2,1,0:T(8,128)S(1)} custom-call(f32[90,48,256]{2,1,0:T(8,128)} %bitcast.3, s32[4,128]{1,0:T(4,128)} %bitcast.5, f32[2,720,384]{2,1,0:T(8,128)} %bitcast.4), custom_call_target="tpu_custom_call" | custom-call | tf_op jit(solution)/shard_map/transform/pallas_call | solution.py:387
  96.0 1.6 %copy.5 = f32[2,720,512]{2,1,0:T(8,128)} copy(f32[2,720,512]{2,1,0:T(8,128)S(1)} %transform.1) | data formatting | bytes 5898240

commit v4 on v3

--- a/solution.py
+++ b/solution.py
@@ -22,7 +22,10 @@
 
 
 LON_STEPS = (
-    (1, 0), (0, 1), (3, 0), (0, 3), (2, 1), (1, 2), (2, 3), (3, 2), (1, 1), (3, 3), (1, 3), (3, 1), (2, 0), (0, 2), (2, 2),
+    (2, 2), (2, 1), (1, 2), (2, 3), (3, 2), (1, 1), (3, 3), (1, 3), (3, 1), (2, 0), (0, 2), (1, 0), (0, 1), (3, 0), (0, 3),
+)
+FAR_LAT_STEPS = (
+    (4, 0), (4, 1), (3, 0), (5, 1), (3, 1), (5, 0), (2, 0), (6, 1), (2, 1), (6, 0), (1, 0), (7, 1), (1, 1), (7, 0), (0, 1),
 )
 LAT_STEPS = (
     (1, 0), (7, 1), (2, 0), (6, 1), (3, 0), (5, 1), (4, 0), (4, 1), (7, 0), (1, 1), (6, 0), (2, 1), (5, 0), (3, 1), (0, 1),
@@ -91,12 +94,10 @@
 
     barrier = pltpu.get_barrier_semaphore()
 
-    def greet(step, _):
-        pl.semaphore_signal(barrier, inc=1, device_id={"lon": lax.rem(lon + step, SECTORS)}, device_id_type=pl.DeviceIdType.MESH)
-        pl.semaphore_signal(barrier, inc=1, device_id={"lat": lax.rem(lat + step, BANDS)}, device_id_type=pl.DeviceIdType.MESH)
-        return 0
-
-    lax.fori_loop(1, 16, greet, 0)
+    for step in LON_STEPS:
+        pl.semaphore_signal(barrier, inc=1, device_id={"lon": lon_peer(step, 1)}, device_id_type=pl.DeviceIdType.MESH)
+    for step in FAR_LAT_STEPS:
+        pl.semaphore_signal(barrier, inc=1, device_id={"lat": lat_peer(step)}, device_id_type=pl.DeviceIdType.MESH)
 
     def arrange(chunk, owner):
         start = jnp.where(northern, owner, 15 - owner)
@@ -373,8 +374,8 @@
     burst(lon_messages(4))
     keep_block(2, 4)
     sum_up(3)
+    sum_up(5)
     sum_up(4)
-    sum_up(5)
     for chunk in range(CHUNKS):
         wait_sent(0, None, chunk)
         wait_sent(1, send_lat, chunk)

time: 99.2 us -> 98.2 us (0.990); the launches traced: 97.6 us -> 98.1 us
  no operation moved by 1% of the time
where the time goes in v4:
time: 98.2 us; the launch traced here: 98.1 us
  Pallas kernels  96.5 us (98%)
  local copies, waits for them, and re-layouts  1.6 us (2%)
    pallas_call x1, Pallas kernels, on_device(): pl.pallas_call(kernel, out_shape=pltpu.VMEM((2, 720, 512), jnp.float32),...  96.5 us

profile of v4, /device:TPU:1, one launch (start us, length us, event | category | flops | bytes accessed | tf_op | source)
XLA Modules:
  0.0 98.1 jit_solution(14588819755205676676)
XLA Ops:
  0.0 96.5 %transform.1 = f32[2,720,512]{2,1,0:T(8,128)S(1)} custom-call(f32[90,48,256]{2,1,0:T(8,128)} %bitcast.3, s32[4,128]{1,0:T(4,128)} %bitcast.5, f32[2,720,384]{2,1,0:T(8,128)} %bitcast.4), custom_call_target="tpu_custom_call" | custom-call | tf_op jit(solution)/shard_map/transform/pallas_call | solution.py:388
  96.5 1.6 %copy.5 = f32[2,720,512]{2,1,0:T(8,128)} copy(f32[2,720,512]{2,1,0:T(8,128)S(1)} %transform.1) | data formatting | bytes 5898240

commit v5 on v4

--- a/solution.py
+++ b/solution.py
@@ -87,17 +87,15 @@
             grid.at[:, pl.ds(first, 16), pl.ds(half * LANES, LANES)], rows_held.at[chunk], row_sems.at[chunk]
         )
 
-    for chunk in range(CHUNKS):
+    load_rows(0).start()
+    barrier = pltpu.get_barrier_semaphore()
+    for lat_step, lon_step in zip(FAR_LAT_STEPS, LON_STEPS):
+        pl.semaphore_signal(barrier, inc=1, device_id={"lat": lat_peer(lat_step)}, device_id_type=pl.DeviceIdType.MESH)
+        pl.semaphore_signal(barrier, inc=1, device_id={"lon": lon_peer(lon_step, 1)}, device_id_type=pl.DeviceIdType.MESH)
+    for chunk in range(1, CHUNKS):
         load_rows(chunk).start()
     table_copy = pltpu.make_async_copy(basis, table, table_sem)
     table_copy.start()
-
-    barrier = pltpu.get_barrier_semaphore()
-
-    for step in LON_STEPS:
-        pl.semaphore_signal(barrier, inc=1, device_id={"lon": lon_peer(step, 1)}, device_id_type=pl.DeviceIdType.MESH)
-    for step in FAR_LAT_STEPS:
-        pl.semaphore_signal(barrier, inc=1, device_id={"lat": lat_peer(step)}, device_id_type=pl.DeviceIdType.MESH)
 
     def arrange(chunk, owner):
         start = jnp.where(northern, owner, 15 - owner)
@@ -307,9 +305,11 @@
             high, low = split(jnp.concatenate(pair, 1))
             kind = THIRDS if late else third
             one_high, one_low = table_high[slot, kind], table_low[slot, kind]
-            sums = jnp.dot(one_high, high, preferred_element_type=jnp.float32)
-            sums += jnp.dot(one_high, low, preferred_element_type=jnp.float32)
-            sums += jnp.dot(one_low, high, preferred_element_type=jnp.float32)
+            sums = jnp.dot(
+                jnp.concatenate([one_high, one_high, one_low], 1),
+                jnp.concatenate([high, low, high], 0),
+                preferred_element_type=jnp.float32,
+            )
             for part in range(2):
                 columns = pl.ds(part * 256 + half * LANES, LANES)
                 piece = sums[:, part * LANES : (part + 1) * LANES]

time: 98.2 us -> 98.1 us (level)
  no operation moved by 1% of the time
where the time goes in v5:
time: 98.1 us; the launch traced here: 98 us
  Pallas kernels  96.4 us (98%)
  local copies, waits for them, and re-layouts  1.6 us (2%)
    pallas_call x1, Pallas kernels, on_device(): pl.pallas_call(kernel, out_shape=pltpu.VMEM((2, 720, 512), jnp.float32),...  96.4 us

profile of v5, /device:TPU:1, one launch (start us, length us, event | category | flops | bytes accessed | tf_op | source)
XLA Modules:
  0.0 98.0 jit_solution(8835377339191829056)
XLA Ops:
  0.0 96.4 %transform.1 = f32[2,720,512]{2,1,0:T(8,128)S(1)} custom-call(f32[90,48,256]{2,1,0:T(8,128)} %bitcast.3, s32[4,128]{1,0:T(4,128)} %bitcast.5, f32[2,720,384]{2,1,0:T(8,128)} %bitcast.4), custom_call_target="tpu_custom_call" | custom-call | tf_op jit(solution)/shard_map/transform/pallas_call | solution.py:388
  96.4 1.6 %copy.5 = f32[2,720,512]{2,1,0:T(8,128)} copy(f32[2,720,512]{2,1,0:T(8,128)S(1)} %transform.1) | data formatting | bytes 5898240

commit v6 on v5

--- a/solution.py
+++ b/solution.py
@@ -84,7 +84,9 @@
         half, third = divmod(chunk, THIRDS)
         first = pl.multiple_of(jnp.where(northern, 16 * third, 32 - 16 * third), 16)
         return pltpu.make_async_copy(
-            grid.at[:, pl.ds(first, 16), pl.ds(half * LANES, LANES)], rows_held.at[chunk], row_sems.at[chunk]
+            grid.at[:, pl.ds(first, 16), pl.ds(half * LANES, LANES)],
+            rows_held.at[chunk, pl.ds(0, 90)],
+            row_sems.at[chunk],
         )
 
     load_rows(0).start()
@@ -99,7 +101,7 @@
 
     def arrange(chunk, owner):
         start = jnp.where(northern, owner, 15 - owner)
-        circles_out[chunk, owner] = rows_held.at[chunk].reshape(90 * 16, LANES)[pl.ds(start, 90, stride=16), :]
+        circles_out[chunk, owner] = rows_held.at[chunk].reshape(SECTOR_ROWS * 16, LANES)[pl.ds(start, 90, stride=16), :]
 
     def send_circle(chunk, peer):
         if chunk:
@@ -391,10 +393,10 @@
         in_specs=[any_space, vmem, any_space],
         out_specs=vmem,
         scratch_shapes=[
-            pltpu.VMEM((CHUNKS, 90, 16, LANES), jnp.float32),
+            pltpu.VMEM((CHUNKS, SECTOR_ROWS, 16, LANES), jnp.float32),
             pltpu.VMEM((CHUNKS, SECTORS, 90, LANES), jnp.float32),
             pltpu.VMEM((CHUNKS, SECTORS, 90, LANES), jnp.float32),
-            pltpu.VMEM((512, LANES), jnp.float32),
+            pltpu.VMEM((520, LANES), jnp.float32),
             pltpu.VMEM((ALL_ROWS, POINTS), jnp.bfloat16),
             pltpu.VMEM((ALL_ROWS, POINTS), jnp.bfloat16),
             pltpu.VMEM((POINTS, 2 * LANES), jnp.bfloat16),

time: 98.1 us -> 98.1 us (level)
  no operation moved by 1% of the time
where the time goes in v6:
time: 98.1 us; the launch traced here: 98 us
  Pallas kernels  96.4 us (98%)
  local copies, waits for them, and re-layouts  1.6 us (2%)
    pallas_call x1, Pallas kernels, on_device(): pl.pallas_call(kernel, out_shape=pltpu.VMEM((2, 720, 512), jnp.float32),...  96.4 us

profile of v6, /device:TPU:1, one launch (start us, length us, event | category | flops | bytes accessed | tf_op | source)
XLA Modules:
  0.0 98.0 jit_solution(13909729553405394331)
XLA Ops:
  0.0 96.4 %transform.1 = f32[2,720,512]{2,1,0:T(8,128)S(1)} custom-call(f32[90,48,256]{2,1,0:T(8,128)} %bitcast.3, s32[4,128]{1,0:T(4,128)} %bitcast.5, f32[2,720,384]{2,1,0:T(8,128)} %bitcast.4), custom_call_target="tpu_custom_call" | custom-call | tf_op jit(solution)/shard_map/transform/pallas_call | solution.py:390
  96.4 1.6 %copy.5 = f32[2,720,512]{2,1,0:T(8,128)} copy(f32[2,720,512]{2,1,0:T(8,128)S(1)} %transform.1) | data formatting | bytes 5898240

commit v7 on v6

--- a/solution.py
+++ b/solution.py
@@ -340,11 +340,11 @@
     keep_circle(2)
     build_table()
     transform(1)
-    burst(lat_messages(1), circle_messages(3), circle_messages(4)[:8])
+    burst(lat_messages(1), circle_messages(3))
     keep_block(1, 1)
     keep_circle(3)
     transform(2)
-    burst(lat_messages(2), circle_messages(4)[8:] + circle_messages(5))
+    burst(lat_messages(2), circle_messages(4) + circle_messages(5))
     keep_block(1, 2)
     keep_circle(4)
     keep_circle(5)
@@ -377,11 +377,13 @@
     keep_block(2, 4)
     sum_up(3)
     sum_up(5)
-    sum_up(4)
     for chunk in range(CHUNKS):
         wait_sent(0, None, chunk)
         wait_sent(1, send_lat, chunk)
-        wait_sent(2, send_lon, chunk)
+        if chunk != 4:
+            wait_sent(2, send_lon, chunk)
+    sum_up(4)
+    wait_sent(2, send_lon, 4)
 
 
 def on_device(grid_values, wave_table, legendre_basis):

time: 98.1 us -> 99.4 us (1.013)
  no operation moved by 1% of the time
where the time goes in v7:
time: 99.4 us; the launch traced here: 98.4 us
  Pallas kernels  96.7 us (97%)
  local copies, waits for them, and re-layouts  1.6 us (2%)
    pallas_call x1, Pallas kernels, on_device(): pl.pallas_call(kernel, out_shape=pltpu.VMEM((2, 720, 512), jnp.float32),...  96.7 us

profile of v7, /device:TPU:1, one launch (start us, length us, event | category | flops | bytes accessed | tf_op | source)
XLA Modules:
  0.0 98.4 jit_solution(14451477130716298388)
XLA Ops:
  0.0 96.7 %transform.1 = f32[2,720,512]{2,1,0:T(8,128)S(1)} custom-call(f32[90,48,256]{2,1,0:T(8,128)} %bitcast.3, s32[4,128]{1,0:T(4,128)} %bitcast.5, f32[2,720,384]{2,1,0:T(8,128)} %bitcast.4), custom_call_target="tpu_custom_call" | custom-call | tf_op jit(solution)/shard_map/transform/pallas_call | solution.py:392
  96.8 1.6 %copy.5 = f32[2,720,512]{2,1,0:T(8,128)} copy(f32[2,720,512]{2,1,0:T(8,128)S(1)} %transform.1) | data formatting | bytes 5898240
